TPU v7x, 256 devices: a whole 4x4x8 slice. The times are simulated.
256 devices in a mesh: section: 4 (over z_lo, core), dp: 64 (over z_hi, y, x).
Axes of the slice: x: 4, y: 4, z: 8 (z_hi: 4, z_lo: 2; z = z_hi * 2 + z_lo), core: 2. Of those that a mesh axis runs over, the one named last changes fastest.
Arguments:
- activations: bfloat16 [4, 4, 3584, 6144], P('section', None, 'dp'), may hold values from -16 to 16
- top_cotangent: bfloat16 [4, 3584, 6144], P(None, 'dp'), may hold values from -16 to 16
- branch_gains: float32 [4, 6144], P('section'), may hold values from 0.5 to 1.5
Outputs:
- input_factor: float32 [4, 6144, 384], P('section', 'dp')
- grad_factor: float32 [4, 6144, 384], P('section', 'dp')
All inputs are finite; a program needn't handle non-finite values.
Results may differ from a plain program's by a relative error of at most 0.0037.
Values may be sent and summed in bfloat16 or wider, within the bound.
A program may use at most 128 MiB of HBM per device.

v0:
```python
import jax
import jax.numpy as jnp
from jax import lax
from jax.sharding import PartitionSpec as P

PANEL = 384


def shifted(value, axis, steps):
    count = lax.axis_size(axis)
    leading, last = (max(0, -steps), min(count, count - steps))
    return lax.ppermute(value, axis, [(source, source + steps) for source in range(leading, last)])


def gelu_slope(values):
    return (
        0.5 * (1.0 + lax.erf(values * 0.7071067811865476))
        + values * jnp.exp(-0.5 * values * values) * 0.3989422804014327
    )


def panel_term(flat_rows, panel_width):
    return jnp.einsum(
        "nr,nc->rc", flat_rows, flat_rows[:, :panel_width], preferred_element_type=jnp.float32
    )


def body(activations, top_cotangent, branch_gains):
    micro_count, token_count, width_all = top_cotangent.shape
    sections = lax.axis_size("section")
    section_index = lax.axis_index("section")
    is_last = section_index == sections - 1
    total_rows = micro_count * token_count * lax.axis_size("dp")
    panel_width = PANEL
    layer_input = activations[0]
    flat_input = layer_input.reshape(micro_count * token_count, width_all)
    scaling = 1.0 + branch_gains[0][None, None, :] * gelu_slope(layer_input.astype(jnp.float32))
    cotangent = top_cotangent
    for hop_number in range(sections - 1):
        outgoing = (cotangent.astype(jnp.float32) * scaling).astype(jnp.bfloat16)
        arrived = shifted(outgoing, "section", -1)
        cotangent = jnp.where(is_last, top_cotangent, arrived)
    flat_cotangent = cotangent.reshape(micro_count * token_count, width_all)
    joined = lax.psum_scatter(
        jnp.concatenate(
            [panel_term(flat_input, panel_width), panel_term(flat_cotangent, panel_width)], axis=1
        ),
        "dp",
        scatter_dimension=0,
        tiled=True,
    )
    input_panel = joined[:, :panel_width]
    grad_panel = joined[:, panel_width:]
    divisor = jnp.float32(total_rows)
    return ((input_panel / divisor)[None], (grad_panel / divisor)[None])


def solution(mesh):
    in_specs = (P("section", None, "dp", None), P(None, "dp", None), P("section", None))
    out_specs = (P("section", "dp", None), P("section", "dp", None))
    return jax.shard_map(body, mesh=mesh, in_specs=in_specs, out_specs=out_specs, check_vma=False)
```

profile of v0, /device:TPU:16, one launch (start us, length us, event | category | flops | bytes accessed | tf_op | source)
XLA Modules:
  0.0 449.1 jit_solution(14333988765760407084)
XLA Ops:
  7.2 0.0 reduce-scatter.4.cloned.1.call-start
  7.2 0.0 copy-start.1
  7.2 8.1 %multiply_convert_fusion.2 = (bf16[4,56,6144]{2,1,0:T(8,128)(2,1)}, f32[4,56,6144]{2,1,0:T(8,128)}) fusion(bf16[4,56,6144]{2,1,0:T(8,128)(2,1)} %param.4, bf16[1,4,56,6144]{3,2,1,0:T(8,128)(2,1)} %param.3, f32[6144]{0:T(1024)} %bitcast.16), kind=kLoop, calls=%fused_computation.15 | loop fusion | flops 19267584 | bytes 13787136 | tf_op jit(solution)/shard_map/convert_element_type | solution.py:40
  15.3 1.3 collective-permute-start
  16.6 6.0 %collective-permute-done = bf16[4,56,6144]{2,1,0:T(8,128)(2,1)} collective-permute-done((bf16[4,56,6144]{2,1,0:T(8,128)(2,1)}, bf16[4,56,6144]{2,1,0:T(8,128)(2,1)}, u32[]{:S(2)}, u32[]{:S(2)}) %collective-permute-start) | collective-permute-done | bytes 2752544 | tf_op jit(solution)/shard_map/ppermute | solution.py:12
  22.6 0.0 copy-done.1
  22.6 0.0 copy-start
  22.6 4.7 %multiply_convert_fusion.1 = bf16[4,56,6144]{2,1,0:T(8,128)(2,1)S(1)} fusion(f32[4,56,6144]{2,1,0:T(8,128)} %get-tuple-element.7, bf16[4,56,6144]{2,1,0:T(8,128)(2,1)S(1)} %copy-done.1, bf16[4,56,6144]{2,1,0:T(8,128)(2,1)} %collective-permute-done, pred[]{:T(512)S(6)} %eq.3), kind=kLoop, calls=%fused_computation.14 | loop fusion | flops 5505024 | bytes 13762561 | tf_op jit(solution)/shard_map/convert_element_type | solution.py:40
  27.3 0.0 copy-start.2
  27.3 1.4 collective-permute-start.1
  28.7 32.9 %collective-permute-done.1 = bf16[4,56,6144]{2,1,0:T(8,128)(2,1)S(1)} collective-permute-done((bf16[4,56,6144]{2,1,0:T(8,128)(2,1)S(1)}, bf16[4,56,6144]{2,1,0:T(8,128)(2,1)S(1)}, u32[]{:S(2)}, u32[]{:S(2)}) %collective-permute-start.1) | collective-permute-done | bytes 2752544 | tf_op jit(solution)/shard_map/ppermute | solution.py:12
  61.6 0.0 copy-done
  61.6 1.3 multiply_convert_fusion
  62.9 1.3 collective-permute-start.2
  64.2 0.0 copy-done.2
  64.2 1.4 fusion.10
  65.6 31.6 %collective-permute-done.2 = bf16[4,56,6144]{2,1,0:T(8,128)(2,1)S(1)} collective-permute-done((bf16[4,56,6144]{2,1,0:T(8,128)(2,1)S(1)}, bf16[4,56,6144]{2,1,0:T(8,128)(2,1)S(1)}, u32[]{:S(2)}, u32[]{:S(2)}) %collective-permute-start.2) | collective-permute-done | bytes 2752544 | tf_op jit(solution)/shard_map/ppermute | solution.py:12
  97.2 0.3 broadcast_select_fusion
  97.5 1.4 fusion.8
  99.0 6.9 %pad_maximum_fusion = f32[6144,768]{0,1:T(8,128)} fusion(f32[6144,384]{0,1:T(8,128)S(1)} %fusion.8, f32[6144,384]{0,1:T(8,128)S(1)} %fusion.10), kind=kLoop, calls=%fused_computation | loop fusion | flops 4718592 | bytes 37748736 | tf_op jit(solution)/shard_map/concatenate | solution.py:45
  105.9 18.6 %copy.9 = f32[6144,768]{1,0:T(8,128)} copy(f32[6144,768]{0,1:T(8,128)} %pad_maximum_fusion) | data formatting | bytes 37748736
  124.6 0.0 reduce-scatter.4.cloned.1.call-update
  124.6 314.8 %reduce-scatter.4.cloned.1.call-done = f32[96,768]{1,0:T(8,128)} async-done(((f32[6144,768]{1,0:T(8,128)}), f32[96,768]{1,0:T(8,128)}) %reduce-scatter.4.cloned.1.call-update) | async-done | bytes 294928
  439.4 1.0 fusion.13
  440.4 0.1 copy.12
  440.5 0.8 copy.8
  441.3 0.1 copy.11
  441.5 0.8 copy.7
  (2 shorter events, 0.0 us)
Async XLA Ops:
  7.2 432.2 %reduce-scatter.4.cloned.1.call-start = ((), (), s32[]{:S(2)}) async-start(), calls=%async_computation.1 | async-start | bytes 19169280
  7.2 15.4 %copy-start.1 = (bf16[4,56,6144]{2,1,0:T(8,128)(2,1)S(1)}, bf16[4,56,6144]{2,1,0:T(8,128)(2,1)}, u32[]{:S(2)}) copy-start(bf16[4,56,6144]{2,1,0:T(8,128)(2,1)} %param.4) | copy-start | bytes 8257540
  15.3 7.3 %collective-permute-start = (bf16[4,56,6144]{2,1,0:T(8,128)(2,1)}, bf16[4,56,6144]{2,1,0:T(8,128)(2,1)}, u32[]{:S(2)}, u32[]{:S(2)}) collective-permute-start(bf16[4,56,6144]{2,1,0:T(8,128)(2,1)} %get-tuple-element.6), channel_id=1, source_target_pairs={{64,0},{128,64},{192,128},{65,1},{129,65},{193,129},{66,2},{130,66... | collective-permute-start | bytes 8257544 | tf_op jit(solution)/shard_map/ppermute | solution.py:12
  22.6 39.0 %copy-start = (f32[4,56,6144]{2,1,0:T(8,128)S(1)}, f32[4,56,6144]{2,1,0:T(8,128)}, u32[]{:S(2)}) copy-start(f32[4,56,6144]{2,1,0:T(8,128)} %get-tuple-element.7) | copy-start | bytes 16515076
  27.3 36.9 %copy-start.2 = (bf16[1,4,56,6144]{3,2,1,0:T(8,128)(2,1)S(1)}, bf16[1,4,56,6144]{3,2,1,0:T(8,128)(2,1)}, u32[]{:S(2)}) copy-start(bf16[1,4,56,6144]{3,2,1,0:T(8,128)(2,1)} %param.3) | copy-start | bytes 8257540
  27.3 34.3 %collective-permute-start.1 = (bf16[4,56,6144]{2,1,0:T(8,128)(2,1)S(1)}, bf16[4,56,6144]{2,1,0:T(8,128)(2,1)S(1)}, u32[]{:S(2)}, u32[]{:S(2)}) collective-permute-start(bf16[4,56,6144]{2,1,0:T(8,128)(2,1)S(1)} %multiply_convert_fusion.1), channel_id=1, source_target_pairs={{64,0},{128,64},{192,128},{65,1},{129,65},{193,129},{66,2},{130,66... | collective-permute-start | bytes 8257544 | tf_op jit(solution)/shard_map/ppermute | solution.py:12
  62.9 34.4 %collective-permute-start.2 = (bf16[4,56,6144]{2,1,0:T(8,128)(2,1)S(1)}, bf16[4,56,6144]{2,1,0:T(8,128)(2,1)S(1)}, u32[]{:S(2)}, u32[]{:S(2)}) collective-permute-start(bf16[4,56,6144]{2,1,0:T(8,128)(2,1)S(1)} %multiply_convert_fusion), channel_id=1, source_target_pairs={{64,0},{128,64},{192,128},{65,1},{129,65},{193,129},{66,2},{130,66... | collective-permute-start | bytes 8257544 | tf_op jit(solution)/shard_map/ppermute | solution.py:12
Sparse Core Ops, SparseCore 0:
  124.7 314.6 reduce-scatter.3
where the time goes:
time: 450 us; the launch traced here: 449 us
  waiting for transfers between devices  385 us (86%)
  local copies, waits for them, and re-layouts  21.5 us (5%)
  other arithmetic  21.3 us (5%)
  between operations  14.1 us (3%)
    unnamed x2, waiting for transfers between devices  315 us
    ppermute x3, waiting for transfers between devices, shifted(): lax.ppermute(value, axis, [(source, source + steps) for source in range(l...  70.5 us
    unnamed x11, local copies, waits for them, and re-layouts  20.5 us
    convert_element_type x3, other arithmetic, body(): outgoing = (cotangent.astype(jnp.float32) * scaling).astype(jnp.bfloat16)  14 us
  transfers between devices with their start and end apart: 4, of which 4 were waited for; matrix products, arithmetic and copies ran while one was open for 0% of the time, Pallas kernels for 0%

commit v1 on v0

v1 whole, which is shorter than its diff:
```python
import jax
import jax.numpy as jnp
from jax import lax
from jax.experimental import pallas as pl
from jax.experimental.pallas import tpu as pltpu
from jax.sharding import PartitionSpec as P

PANEL = 384
ROWS = 224
BLOCKS = 16
SLAB = 32
MESH = pl.DeviceIdType.MESH
F32 = jnp.float32
BF16 = jnp.bfloat16


def gelu_slope(values):
    return (
        0.5 * (1.0 + lax.erf(values * 0.7071067811865476))
        + values * jnp.exp(-0.5 * values * values) * 0.3989422804014327
    )


def kernel(
    total_rows,
    x_hbm,
    top_hbm,
    gains,
    in_out,
    grad_out,
    xbuf,
    cbuf,
    obuf,
    held,
    part,
    bsend,
    brecv,
    csend,
    crecv,
    fin,
    x_load,
    c_in,
    relay_sent,
    a_sent,
    a_in,
    b_sent,
    b_in,
    c_sent,
    c_got,
):
    s = lax.axis_index("section")
    d = lax.axis_index("dp")
    core = s % 2
    zh, y, x = d // 16, (d // 4) % 4, d % 4
    a = jnp.where(core == 0, y, x)
    b = jnp.where(core == 0, x, y)

    def at(zz, aa, bb):
        return zz * 16 + jnp.where(core == 0, aa * 4 + bb, bb * 4 + aa)

    def peer_a(aa):
        return (s, at(zh, aa, b))

    def peer_b(bb):
        return (s, at(zh, a, bb))

    def owner(zz):
        return (s, zz * 16 + a * 4 + b)

    swapped = jnp.logical_and(core == 1, a != b)
    straight = jnp.logical_not(swapped)

    barrier = pltpu.get_barrier_semaphore()

    def greet(device):
        pl.semaphore_signal(barrier, inc=1, device_id=device, device_id_type=MESH)

    for o in (1, 2, 3):
        greet(peer_a((a + o) % 4))
        greet(peer_b((b + o) % 4))
        greet(owner((zh + o) % 4))

    @pl.when(swapped)
    def _():
        greet(owner(zh))

    @pl.when(s > 0)
    def _():
        greet((s - 1, d))

    @pl.when(s < 3)
    def _():
        greet((s + 1, d))

    first = 4 * (3 - zh) + (8 - x - y) % 4

    def block_at(p):
        i = jnp.where(p == 0, first, jnp.where(p <= first, p - 1, p))
        return ((zh + 1 + i // 4) % 4) * 4 + (i + x + y) % 4

    def columns(blk):
        return pl.ds(pl.multiple_of(blk * PANEL, PANEL), PANEL)

    def rows_of(aa):
        return pl.ds(pl.multiple_of(aa * ROWS, ROWS), ROWS)

    def load(p, _):
        blk = block_at(p)

        @pl.when(s > 0)
        def _():
            pltpu.make_async_copy(x_hbm.at[:, columns(blk)], xbuf.at[blk], x_load.at[blk]).start()

        @pl.when(s == 3)
        def _():
            pltpu.make_async_copy(top_hbm.at[:, columns(blk)], cbuf.at[blk], c_in.at[blk]).start()

        return 0

    lax.fori_loop(0, BLOCKS, load, 0)

    others = 9 + jnp.where(swapped, 1, 0) + jnp.where(s > 0, 1, 0) + jnp.where(s < 3, 1, 0)
    pl.semaphore_wait(barrier, others)

    def to_peer(f, src, slot, sent, aa):
        return pltpu.make_async_remote_copy(
            src_ref=src,
            dst_ref=held.at[f, slot, rows_of(a), :],
            send_sem=a_sent.at[f, sent],
            recv_sem=a_in.at[f, slot, a],
            device_id=peer_a(aa),
            device_id_type=MESH,
        )

    def keep(f, src, slot):
        return pltpu.make_async_copy(src, held.at[f, slot, rows_of(a), :], a_in.at[f, slot, a])

    def sends_block(zz, aa):
        return jnp.logical_or(zz != 0, aa != 0)

    panel_src = x_hbm.at[:, pl.ds(0, PANEL)]
    for o in (2, 1, 3):
        to_peer(0, panel_src, 4, 16 + o, (a + o) % 4).start()
    keep(0, panel_src, 4).start()

    def send_x(j, _):
        zz = (zh + 1 + j) % 4
        for o in (2, 1, 3):
            aa = (a + o) % 4
            blk = zz * 4 + aa

            @pl.when(sends_block(zz, aa))
            def _():
                to_peer(0, x_hbm.at[:, columns(blk)], zz, blk, aa).start()

        @pl.when(sends_block(zz, a))
        def _():
            keep(0, x_hbm.at[:, columns(zz * 4 + a)], zz).start()

        return 0

    lax.fori_loop(0, 4, send_x, 0)

    def relay_copy(blk):
        return pltpu.make_async_remote_copy(
            src_ref=obuf.at[blk],
            dst_ref=cbuf.at[blk],
            send_sem=relay_sent.at[blk],
            recv_sem=c_in.at[blk],
            device_id=(s - 1, d),
            device_id_type=MESH,
        )

    def relay(p, _):
        blk = block_at(p)
        zz, q = blk // 4, blk % 4
        pltpu.make_async_copy(cbuf.at[blk], cbuf.at[blk], c_in.at[blk]).wait()

        @pl.when(p == 0)
        def _():
            for o in (2, 1, 3):
                to_peer(1, cbuf.at[blk], 4, 16 + o, (a + o) % 4).start()
            keep(1, cbuf.at[blk], 4).start()

        @pl.when(jnp.logical_and(p > 0, q != a))
        def _():
            to_peer(1, cbuf.at[blk], zz, blk, q).start()

        @pl.when(jnp.logical_and(p > 0, q == a))
        def _():
            keep(1, cbuf.at[blk], zz).start()

        @pl.when(s > 0)
        def _():
            pltpu.make_async_copy(xbuf.at[blk], xbuf.at[blk], x_load.at[blk]).wait()
            gain = gains[blk]

            def slab(i, _):
                rows = pl.ds(pl.multiple_of(i * SLAB, SLAB), SLAB)
                scaling = 1.0 + gain * gelu_slope(xbuf[blk, rows, :].astype(F32))
                obuf[blk, rows, :] = (cbuf[blk, rows, :].astype(F32) * scaling).astype(BF16)
                return 0

            lax.fori_loop(0, ROWS // SLAB, slab, 0)
            relay_copy(blk).start()

        return 0

    def await_slot(f, slot):
        for aa in range(4):
            there = held.at[f, slot, pl.ds(aa * ROWS, ROWS), :]
            pltpu.make_async_copy(there, there, a_in.at[f, slot, aa]).wait()

    def b_copy(f, j, o):
        bb = (b + o) % 4
        return pltpu.make_async_remote_copy(
            src_ref=bsend.at[f, j, bb],
            dst_ref=brecv.at[f, j, o - 1],
            send_sem=b_sent.at[f, j, o - 1],
            recv_sem=b_in.at[f, j, o - 1],
            device_id=peer_b(bb),
            device_id_type=MESH,
        )

    def gram(f, j):
        zz = (zh + 1 + j) % 4
        slot = jnp.where(sends_block(zz, a), zz, 4)
        if j == 0:
            await_slot(f, 4)

        @pl.when(sends_block(zz, a))
        def _():
            await_slot(f, zz)

        part[f, j] = lax.dot_general(
            held[f, slot], held[f, 4], (((0,), (0,)), ((), ())), preferred_element_type=F32
        )
        for bb in range(4):
            bsend[f, j, bb] = part[f, j, pl.ds(bb * 96, 96), :].astype(BF16)
        for o in (2, 1, 3):
            b_copy(f, j, o).start()

    def c_copy(f, j):
        return pltpu.make_async_remote_copy(
            src_ref=csend.at[f, j],
            dst_ref=crecv.at[f, j],
            send_sem=c_sent.at[f, j],
            recv_sem=c_got.at[f, j],
            device_id=owner((zh + 1 + j) % 4),
            device_id_type=MESH,
        )

    def sum_b(f, j):
        total = part[f, j, pl.ds(pl.multiple_of(b * 96, 96), 96), :]
        for o in (1, 3, 2):
            b_copy(f, j, o).wait_recv()
            total = total + brecv[f, j, o - 1].astype(F32)
        if j < 3:
            csend[f, j] = total.astype(BF16)
            c_copy(f, j).start()
        else:
            fin[f] = total

            @pl.when(swapped)
            def _():
                csend[f, j] = total.astype(BF16)
                c_copy(f, j).start()

    def finish(f, out):
        @pl.when(swapped)
        def _():
            c_copy(f, 3).wait_recv()
            fin[f] = crecv[f, 3].astype(F32)

        total = fin[f]
        for j in range(3):
            c_copy(f, j).wait_recv()
            total = total + crecv[f, j].astype(F32)
        out[0] = total / F32(total_rows)

    def relays(low, high):
        lax.fori_loop(low, high, relay, 0)

    relays(0, 7)
    gram(0, 0)
    relays(7, 9)
    gram(0, 1)
    sum_b(0, 0)
    relays(9, 11)
    gram(0, 2)
    sum_b(0, 1)
    relays(11, 13)
    gram(0, 3)
    gram(1, 0)
    sum_b(0, 2)
    relays(13, 15)
    gram(1, 1)
    sum_b(0, 3)
    relays(15, 16)
    sum_b(1, 0)
    gram(1, 2)
    sum_b(1, 1)
    finish(0, in_out)
    gram(1, 3)
    sum_b(1, 2)
    sum_b(1, 3)
    finish(1, grad_out)

    for f in range(2):
        for o in (1, 2, 3):
            to_peer(f, cbuf.at[0], 4, 16 + o, (a + o) % 4).wait_send()

        def sent(blk, _):
            q = blk % 4

            @pl.when(jnp.logical_and(blk > 0, q != a))
            def _():
                to_peer(f, cbuf.at[blk], blk // 4, blk, q).wait_send()

            return 0

        lax.fori_loop(0, BLOCKS, sent, 0)
        for j in range(4):
            for o in (1, 2, 3):
                b_copy(f, j, o).wait_send()
        for j in range(3):
            c_copy(f, j).wait_send()

        @pl.when(swapped)
        def _():
            c_copy(f, 3).wait_send()

    @pl.when(s > 0)
    def _():
        def relayed(blk, _):
            relay_copy(blk).wait_send()
            return 0

        lax.fori_loop(0, BLOCKS, relayed, 0)


def body(activations, top_cotangent, branch_gains):
    width = activations.shape[-1]
    total_rows = ROWS * lax.axis_size("dp")
    dma = pltpu.SemaphoreType.DMA
    return pl.pallas_call(
        lambda *refs: kernel(total_rows, *refs),
        out_shape=[jax.ShapeDtypeStruct((1, 96, PANEL), F32)] * 2,
        in_specs=[
            pl.BlockSpec(memory_space=pl.ANY),
            pl.BlockSpec(memory_space=pl.ANY),
            pl.BlockSpec(memory_space=pltpu.VMEM),
        ],
        out_specs=[pl.BlockSpec(memory_space=pltpu.VMEM)] * 2,
        scratch_shapes=[
            pltpu.VMEM((BLOCKS, ROWS, PANEL), BF16),
            pltpu.VMEM((BLOCKS, ROWS, PANEL), BF16),
            pltpu.VMEM((BLOCKS, ROWS, PANEL), BF16),
            pltpu.VMEM((2, 5, 4 * ROWS, PANEL), BF16),
            pltpu.VMEM((2, 4, PANEL, PANEL), F32),
            pltpu.VMEM((2, 4, 4, 96, PANEL), BF16),
            pltpu.VMEM((2, 4, 3, 96, PANEL), BF16),
            pltpu.VMEM((2, 4, 96, PANEL), BF16),
            pltpu.VMEM((2, 4, 96, PANEL), BF16),
            pltpu.VMEM((2, 96, PANEL), F32),
            dma((BLOCKS,)),
            dma((BLOCKS,)),
            dma((BLOCKS,)),
            dma((2, 20)),
            dma((2, 5, 4)),
            dma((2, 4, 3)),
            dma((2, 4, 3)),
            dma((2, 4)),
            dma((2, 4)),
        ],
        compiler_params=pltpu.CompilerParams(
            collective_id=0, has_side_effects=True, vmem_limit_bytes=48 * 2**20
        ),
        cost_estimate=pl.CostEstimate(
            flops=4 * ROWS * width * PANEL,
            bytes_accessed=4 * ROWS * width,
            transcendentals=2 * ROWS * width,
        ),
    )(
        activations.reshape(ROWS, width),
        top_cotangent.reshape(ROWS, width),
        branch_gains.reshape(BLOCKS, 1, PANEL),
    )


def solution(mesh):
    in_specs = (P("section", None, "dp", None), P(None, "dp", None), P("section", None))
    out_specs = (P("section", "dp", None), P("section", "dp", None))
    return jax.shard_map(
        lambda *args: tuple(body(*args)),
        mesh=mesh,
        in_specs=in_specs,
        out_specs=out_specs,
        check_vma=False,
    )
```

time: 450 us -> 93.4 us (0.21)
  the two profiles are of different devices: /device:TPU:16 before, /device:TPU:14 now
where the time goes in v1:
time: 93.4 us; the launch traced here: 93.2 us
  Pallas kernels  86.9 us (93%)
  local copies, waits for them, and re-layouts  5.61 us (6%)
    pallas_call x1, Pallas kernels, body(): pl.pallas_call(lambda *refs: kernel(total_rows, *refs), out_shape=[jax.Sh...  86.9 us
    unnamed x8, local copies, waits for them, and re-layouts  5.61 us

profile of v1, /device:TPU:14, one launch (start us, length us, event | category | flops | bytes accessed | tf_op | source)
XLA Modules:
  0.0 93.2 jit_solution(11430320335121659387)
XLA Ops:
  0.6 0.0 copy-start
  0.6 1.8 %copy-done = bf16[1,4,56,6144]{3,2,1,0:T(8,128)(2,1)S(1)} copy-done((bf16[1,4,56,6144]{3,2,1,0:T(8,128)(2,1)S(1)}, bf16[1,4,56,6144]{3,2,1,0:T(8,128)(2,1)}, u32[]{:S(2)}) %copy-start) | copy-done | bytes 2752536
  2.4 0.0 copy-start.1
  2.4 1.8 %copy-done.1 = bf16[4,56,6144]{2,1,0:T(8,128)(2,1)S(1)} copy-done((bf16[4,56,6144]{2,1,0:T(8,128)(2,1)S(1)}, bf16[4,56,6144]{2,1,0:T(8,128)(2,1)}, u32[]{:S(2)}) %copy-start.1) | copy-done | bytes 2752536
  4.2 0.0 copy-start.2
  4.2 0.7 copy-done.2
  4.9 86.9 %shard_map.50 = (f32[1,96,384]{2,1,0:T(8,128)S(1)}, f32[1,96,384]{2,1,0:T(8,128)S(1)}) custom-call(bf16[224,6144]{1,0:T(8,128)(2,1)S(1)} %bitcast.3, bf16[224,6144]{1,0:T(8,128)(2,1)S(1)} %bitcast.4, f32[16,1,384]{2,1,0:T(1,128)S(1)} %bitcast.5), custom_call_target="tpu_custom_call" | custom-call | flops 2113929216 | bytes 5505024 | tf_op jit(solution)/shard_map/pallas_call | solution.py:346
  91.9 0.7 copy.7
  92.5 0.7 copy.8
Async XLA Ops:
  0.6 1.8 %copy-start = (bf16[1,4,56,6144]{3,2,1,0:T(8,128)(2,1)S(1)}, bf16[1,4,56,6144]{3,2,1,0:T(8,128)(2,1)}, u32[]{:S(2)}) copy-start(bf16[1,4,56,6144]{3,2,1,0:T(8,128)(2,1)} %param.3) | copy-start | bytes 8257540
  2.4 1.8 %copy-start.1 = (bf16[4,56,6144]{2,1,0:T(8,128)(2,1)S(1)}, bf16[4,56,6144]{2,1,0:T(8,128)(2,1)}, u32[]{:S(2)}) copy-start(bf16[4,56,6144]{2,1,0:T(8,128)(2,1)} %param.4) | copy-start | bytes 8257540
  4.2 0.7 copy-start.2

commit v2 on v1

--- a/solution.py
+++ b/solution.py
@@ -9,6 +9,9 @@
 ROWS = 224
 BLOCKS = 16
 SLAB = 32
+SORTED = 112
+JOBS = (0, 1, 2, 4, 3, 5, 6, 7)
+RELAYED = (3, 6, 9, 10, 12, 14, 16, 16, 16)
 MESH = pl.DeviceIdType.MESH
 F32 = jnp.float32
 BF16 = jnp.bfloat16
@@ -22,14 +25,14 @@
 
 
 def kernel(
-    total_rows,
     x_hbm,
     top_hbm,
-    gains,
+    gains_hbm,
     in_out,
     grad_out,
-    xbuf,
-    cbuf,
+    gains,
+    whole,
+    sorted_by_x,
     obuf,
     held,
     part,
@@ -38,6 +41,7 @@
     csend,
     crecv,
     fin,
+    gain_load,
     x_load,
     c_in,
     relay_sent,
@@ -65,10 +69,9 @@
         return (s, at(zh, a, bb))
 
     def owner(zz):
-        return (s, zz * 16 + a * 4 + b)
-
-    swapped = jnp.logical_and(core == 1, a != b)
-    straight = jnp.logical_not(swapped)
+        return (s, at(zz, a, b))
+
+    xbuf, cbuf = whole.at[0], whole.at[1]
 
     barrier = pltpu.get_barrier_semaphore()
 
@@ -80,10 +83,6 @@
         greet(peer_b((b + o) % 4))
         greet(owner((zh + o) % 4))
 
-    @pl.when(swapped)
-    def _():
-        greet(owner(zh))
-
     @pl.when(s > 0)
     def _():
         greet((s - 1, d))
@@ -118,8 +117,9 @@
         return 0
 
     lax.fori_loop(0, BLOCKS, load, 0)
-
-    others = 9 + jnp.where(swapped, 1, 0) + jnp.where(s > 0, 1, 0) + jnp.where(s < 3, 1, 0)
+    pltpu.make_async_copy(gains_hbm, gains, gain_load).start()
+
+    others = 9 + jnp.where(s > 0, 1, 0) + jnp.where(s < 3, 1, 0)
     pl.semaphore_wait(barrier, others)
 
     def to_peer(f, src, slot, sent, aa):
@@ -136,30 +136,61 @@
         return pltpu.make_async_copy(src, held.at[f, slot, rows_of(a), :], a_in.at[f, slot, a])
 
     def sends_block(zz, aa):
-        return jnp.logical_or(zz != 0, aa != 0)
+        return jnp.logical_or(core == 1, jnp.logical_or(zz != 0, aa != 0))
+
+    def sort_and_send(f, j):
+        zz = (zh + 1 + j) % 4
+
+        def sort(i, _):
+            rows = pl.ds(pl.multiple_of(i * SORTED, SORTED), SORTED)
+            blocks = [whole[f, zz * 4 + yy, rows, :].astype(F32) for yy in range(4)]
+            for xx in range(4):
+                sorted_by_x[f, zz * 4 + xx, rows, :] = jnp.concatenate(
+                    [block[:, xx * 96 : xx * 96 + 96] for block in blocks], axis=1
+                ).astype(BF16)
+            return 0
+
+        lax.fori_loop(0, ROWS // SORTED, sort, 0)
+        for o in (2, 1, 3):
+            aa = (a + o) % 4
+            to_peer(f, sorted_by_x.at[f, zz * 4 + aa], zz, zz * 4 + aa, aa).start()
+        keep(f, sorted_by_x.at[f, zz * 4 + a], zz).start()
 
     panel_src = x_hbm.at[:, pl.ds(0, PANEL)]
     for o in (2, 1, 3):
         to_peer(0, panel_src, 4, 16 + o, (a + o) % 4).start()
     keep(0, panel_src, 4).start()
 
+    def await_x(blk):
+        pltpu.make_async_copy(xbuf.at[blk], xbuf.at[blk], x_load.at[blk]).wait()
+
     def send_x(j, _):
         zz = (zh + 1 + j) % 4
-        for o in (2, 1, 3):
-            aa = (a + o) % 4
-            blk = zz * 4 + aa
-
-            @pl.when(sends_block(zz, aa))
+
+        @pl.when(core == 0)
+        def _():
+            for o in (2, 1, 3):
+                aa = (a + o) % 4
+                blk = zz * 4 + aa
+
+                @pl.when(sends_block(zz, aa))
+                def _():
+                    to_peer(0, x_hbm.at[:, columns(blk)], zz, blk, aa).start()
+
+            @pl.when(sends_block(zz, a))
             def _():
-                to_peer(0, x_hbm.at[:, columns(blk)], zz, blk, aa).start()
-
-        @pl.when(sends_block(zz, a))
-        def _():
-            keep(0, x_hbm.at[:, columns(zz * 4 + a)], zz).start()
+                keep(0, x_hbm.at[:, columns(zz * 4 + a)], zz).start()
+
+        @pl.when(core == 1)
+        def _():
+            for yy in range(4):
+                await_x(zz * 4 + yy)
+            sort_and_send(0, j)
 
         return 0
 
     lax.fori_loop(0, 4, send_x, 0)
+    pltpu.make_async_copy(gains_hbm, gains, gain_load).wait()
 
     def relay_copy(blk):
         return pltpu.make_async_remote_copy(
@@ -182,17 +213,22 @@
                 to_peer(1, cbuf.at[blk], 4, 16 + o, (a + o) % 4).start()
             keep(1, cbuf.at[blk], 4).start()
 
-        @pl.when(jnp.logical_and(p > 0, q != a))
+        straight = jnp.logical_and(core == 0, p > 0)
+
+        @pl.when(jnp.logical_and(straight, q != a))
         def _():
             to_peer(1, cbuf.at[blk], zz, blk, q).start()
 
-        @pl.when(jnp.logical_and(p > 0, q == a))
+        @pl.when(jnp.logical_and(straight, q == a))
         def _():
             keep(1, cbuf.at[blk], zz).start()
 
         @pl.when(s > 0)
         def _():
-            pltpu.make_async_copy(xbuf.at[blk], xbuf.at[blk], x_load.at[blk]).wait()
+            @pl.when(core == 0)
+            def _():
+                await_x(blk)
+
             gain = gains[blk]
 
             def slab(i, _):
@@ -203,6 +239,13 @@
 
             lax.fori_loop(0, ROWS // SLAB, slab, 0)
             relay_copy(blk).start()
+
+        early = first // 4
+        ends = jnp.where(p % 4 == 3, p // 4 >= early, jnp.logical_and(p % 4 == 0, (p + 3) // 4 - 1 < early))
+
+        @pl.when(jnp.logical_and(jnp.logical_and(core == 1, p > 0), ends))
+        def _():
+            sort_and_send(1, (p - 3) // 4)
 
         return 0
 
@@ -225,7 +268,9 @@
     def gram(f, j):
         zz = (zh + 1 + j) % 4
         slot = jnp.where(sends_block(zz, a), zz, 4)
-        if j == 0:
+
+        @pl.when(j == 0)
+        def _():
             await_slot(f, 4)
 
         @pl.when(sends_block(zz, a))
@@ -255,55 +300,55 @@
         for o in (1, 3, 2):
             b_copy(f, j, o).wait_recv()
             total = total + brecv[f, j, o - 1].astype(F32)
-        if j < 3:
+
+        @pl.when(j == 3)
+        def _():
+            fin[f] = total
+
+        @pl.when(j < 3)
+        def _():
             csend[f, j] = total.astype(BF16)
             c_copy(f, j).start()
-        else:
-            fin[f] = total
-
-            @pl.when(swapped)
-            def _():
-                csend[f, j] = total.astype(BF16)
-                c_copy(f, j).start()
 
     def finish(f, out):
-        @pl.when(swapped)
-        def _():
-            c_copy(f, 3).wait_recv()
-            fin[f] = crecv[f, 3].astype(F32)
-
         total = fin[f]
         for j in range(3):
             c_copy(f, j).wait_recv()
             total = total + crecv[f, j].astype(F32)
-        out[0] = total / F32(total_rows)
-
-    def relays(low, high):
-        lax.fori_loop(low, high, relay, 0)
-
-    relays(0, 7)
-    gram(0, 0)
-    relays(7, 9)
-    gram(0, 1)
-    sum_b(0, 0)
-    relays(9, 11)
-    gram(0, 2)
-    sum_b(0, 1)
-    relays(11, 13)
-    gram(0, 3)
-    gram(1, 0)
-    sum_b(0, 2)
-    relays(13, 15)
-    gram(1, 1)
-    sum_b(0, 3)
-    relays(15, 16)
-    sum_b(1, 0)
-    gram(1, 2)
-    sum_b(1, 1)
+        out[...] = total
+
+    upper = s >= 2
+
+    def pick(table, t):
+        value = jnp.int32(table[-1])
+        for i in range(len(table) - 1):
+            value = jnp.where(t == i, table[i], value)
+        return value
+
+    def job_at(t):
+        return jnp.where(upper, t, pick(JOBS, t))
+
+    def relayed_by(t):
+        return jnp.where(upper, BLOCKS, pick(RELAYED, t))
+
+    def step(t, done):
+        upto = relayed_by(t)
+        lax.fori_loop(done, upto, relay, 0)
+
+        @pl.when(t < 8)
+        def _():
+            job = job_at(t)
+            gram(job // 4, job % 4)
+
+        @pl.when(t > 0)
+        def _():
+            job = job_at(t - 1)
+            sum_b(job // 4, job % 4)
+
+        return upto
+
+    lax.fori_loop(0, 9, step, jnp.int32(0))
     finish(0, in_out)
-    gram(1, 3)
-    sum_b(1, 2)
-    sum_b(1, 3)
     finish(1, grad_out)
 
     for f in range(2):
@@ -313,7 +358,7 @@
         def sent(blk, _):
             q = blk % 4
 
-            @pl.when(jnp.logical_and(blk > 0, q != a))
+            @pl.when(jnp.logical_and(sends_block(blk // 4, q), q != a))
             def _():
                 to_peer(f, cbuf.at[blk], blk // 4, blk, q).wait_send()
 
@@ -326,10 +371,6 @@
         for j in range(3):
             c_copy(f, j).wait_send()
 
-        @pl.when(swapped)
-        def _():
-            c_copy(f, 3).wait_send()
-
     @pl.when(s > 0)
     def _():
         def relayed(blk, _):
@@ -343,26 +384,28 @@
     width = activations.shape[-1]
     total_rows = ROWS * lax.axis_size("dp")
     dma = pltpu.SemaphoreType.DMA
-    return pl.pallas_call(
-        lambda *refs: kernel(total_rows, *refs),
-        out_shape=[jax.ShapeDtypeStruct((1, 96, PANEL), F32)] * 2,
+    sums = pl.pallas_call(
+        kernel,
+        out_shape=[jax.ShapeDtypeStruct((96, PANEL), F32)] * 2,
         in_specs=[
             pl.BlockSpec(memory_space=pl.ANY),
             pl.BlockSpec(memory_space=pl.ANY),
-            pl.BlockSpec(memory_space=pltpu.VMEM),
+            pl.BlockSpec(memory_space=pl.ANY),
         ],
         out_specs=[pl.BlockSpec(memory_space=pltpu.VMEM)] * 2,
         scratch_shapes=[
-            pltpu.VMEM((BLOCKS, ROWS, PANEL), BF16),
-            pltpu.VMEM((BLOCKS, ROWS, PANEL), BF16),
+            pltpu.VMEM((BLOCKS, 1, PANEL), F32),
+            pltpu.VMEM((2, BLOCKS, ROWS, PANEL), BF16),
+            pltpu.VMEM((2, BLOCKS, ROWS, PANEL), BF16),
             pltpu.VMEM((BLOCKS, ROWS, PANEL), BF16),
             pltpu.VMEM((2, 5, 4 * ROWS, PANEL), BF16),
             pltpu.VMEM((2, 4, PANEL, PANEL), F32),
             pltpu.VMEM((2, 4, 4, 96, PANEL), BF16),
             pltpu.VMEM((2, 4, 3, 96, PANEL), BF16),
-            pltpu.VMEM((2, 4, 96, PANEL), BF16),
-            pltpu.VMEM((2, 4, 96, PANEL), BF16),
+            pltpu.VMEM((2, 3, 96, PANEL), BF16),
+            pltpu.VMEM((2, 3, 96, PANEL), BF16),
             pltpu.VMEM((2, 96, PANEL), F32),
+            dma,
             dma((BLOCKS,)),
             dma((BLOCKS,)),
             dma((BLOCKS,)),
@@ -370,11 +413,11 @@
             dma((2, 5, 4)),
             dma((2, 4, 3)),
             dma((2, 4, 3)),
-            dma((2, 4)),
-            dma((2, 4)),
+            dma((2, 3)),
+            dma((2, 3)),
         ],
         compiler_params=pltpu.CompilerParams(
-            collective_id=0, has_side_effects=True, vmem_limit_bytes=48 * 2**20
+            collective_id=0, has_side_effects=True, vmem_limit_bytes=56 * 2**20
         ),
         cost_estimate=pl.CostEstimate(
             flops=4 * ROWS * width * PANEL,
@@ -386,13 +429,14 @@
         top_cotangent.reshape(ROWS, width),
         branch_gains.reshape(BLOCKS, 1, PANEL),
     )
+    return tuple((total / F32(total_rows))[None] for total in sums)
 
 
 def solution(mesh):
     in_specs = (P("section", None, "dp", None), P(None, "dp", None), P("section", None))
     out_specs = (P("section", "dp", None), P("section", "dp", None))
     return jax.shard_map(
-        lambda *args: tuple(body(*args)),
+        body,
         mesh=mesh,
         in_specs=in_specs,
         out_specs=out_specs,

time: 93.4 us -> 73.3 us (0.78)
  the two profiles are of different devices: /device:TPU:14 before, /device:TPU:80 now
where the time goes in v2:
time: 73.3 us; the launch traced here: 73.2 us
  Pallas kernels  70.8 us (97%)
  other arithmetic  1.72 us (2%)
    pallas_call x1, Pallas kernels, body(): pl.pallas_call(kernel, out_shape=[jax.ShapeDtypeStruct((96, PANEL), F32)]...  70.8 us
    broadcast_in_dim x1, other arithmetic, body(): return tuple(((total / F32(total_rows))[None] for total in sums))  1.72 us

profile of v2, /device:TPU:80, one launch (start us, length us, event | category | flops | bytes accessed | tf_op | source)
XLA Modules:
  0.0 73.2 jit_solution(14553581861466163396)
XLA Ops:
  0.6 70.8 %shard_map.50 = (f32[96,384]{1,0:T(8,128)}, f32[96,384]{1,0:T(8,128)}) custom-call(bf16[224,6144]{1,0:T(8,128)(2,1)} %bitcast.7, bf16[224,6144]{1,0:T(8,128)(2,1)} %bitcast.8, f32[16,1,384]{2,1,0:T(1,128)} %bitcast.9), custom_call_target="tpu_custom_call" | custom-call | flops 2113929216 | bytes 5505024 | tf_op jit(solution)/shard_map/pallas_call | solution.py:387
  71.4 1.7 %multiply_bitcast_fusion = (f32[1,96,384]{2,1,0:T(8,128)}, f32[1,96,384]{2,1,0:T(8,128)}) fusion(f32[96,384]{1,0:T(8,128)} %get-tuple-element.5, f32[96,384]{1,0:T(8,128)} %get-tuple-element.4), kind=kLoop, calls=%fused_computation | loop fusion | flops 73728 | bytes 589824 | tf_op jit(solution)/shard_map/broadcast_in_dim | solution.py:432

commit v3 on v2

v3 whole, which is shorter than its diff:
```python
import jax
import jax.numpy as jnp
from jax import lax
from jax.experimental import pallas as pl
from jax.experimental.pallas import tpu as pltpu
from jax.sharding import PartitionSpec as P

PANEL = 384
ROWS = 224
BLOCKS = 16
SLAB = 32
SORTED = 112
KINDS = RELAY, HAND_C, GRAM_X, GRAM_C, SUM_A, SUM_B, MEET, SWAP_X = range(8)
R, S, G, D, A, B, M, X = (32 * kind for kind in KINDS)
SECTION3 = (R + 2, X + 0, R + 4, X + 1, R + 6, X + 2, R + 8, X + 3, R + 16, G + 0, G + 1, S + 0, S + 1, G + 2, G + 3, S + 2, S + 3, A + 0, A + 1, A + 2, A + 3, D + 0, D + 1, M + 0, B + 0, B + 1, B + 2, B + 3, D + 2, D + 3, B + 4, B + 5, B + 6, B + 7)
SECTION2 = (X + 0, X + 1, X + 2, X + 3, R + 16, G + 0, G + 1, S + 0, S + 1, G + 2, G + 3, S + 2, S + 3, A + 0, A + 1, A + 2, A + 3, D + 0, D + 1, M + 0, B + 0, B + 1, B + 2, B + 3, D + 2, D + 3, B + 4, B + 5, B + 6, B + 7)
SECTION1 = (X + 0, X + 1, X + 2, X + 3, R + 4, G + 0, G + 1, R + 5, S + 0, G + 2, G + 3, R + 9, S + 1, A + 0, A + 1, D + 0, R + 10, A + 2, A + 3, R + 13, S + 2, D + 1, M + 0, B + 0, B + 1, B + 4, R + 16, S + 3, B + 2, B + 3, D + 2, B + 5, D + 3, B + 6, B + 7)
SECTION0 = (X + 0, X + 1, X + 2, X + 3, R + 4, G + 0, G + 1, R + 5, S + 0, G + 2, G + 3, R + 9, S + 1, A + 0, A + 1, D + 0, R + 10, A + 2, A + 3, R + 13, S + 2, D + 1, M + 0, B + 0, B + 1, B + 4, R + 16, S + 3, B + 2, B + 3, D + 2, B + 5, D + 3, B + 6, B + 7)
WORDS = 15
MESH = pl.DeviceIdType.MESH
F32 = jnp.float32
BF16 = jnp.bfloat16


def packed(ops):
    codes = ops + (R + BLOCKS,) * (3 * WORDS - len(ops))
    return [codes[i] + 256 * codes[i + 1] + 65536 * codes[i + 2] for i in range(0, len(codes), 3)]


def gelu_slope(values):
    return (
        0.5 * (1.0 + lax.erf(values * 0.7071067811865476))
        + values * jnp.exp(-0.5 * values * values) * 0.3989422804014327
    )


def kernel(
    x_hbm,
    top_hbm,
    gains_hbm,
    in_out,
    grad_out,
    gains,
    whole,
    sorted_by_x,
    obuf,
    held,
    gathered,
    part,
    asend,
    arecv,
    bsend,
    brecv,
    csend,
    crecv,
    fin,
    gain_load,
    x_load,
    c_in,
    relay_sent,
    swap_sent,
    swap_in,
    gather_sent,
    gather_in,
    a_sent,
    a_in,
    b_sent,
    b_in,
    c_sent,
    c_got,
    above,
):
    s = lax.axis_index("section")
    d = lax.axis_index("dp")
    core = s % 2
    zh, y, x = d // 16, (d // 4) % 4, d % 4
    a = jnp.where(core == 0, y, x)
    b = jnp.where(core == 0, x, y)
    xbuf, cbuf = whole.at[0], whole.at[1]

    def at(zz, aa, bb):
        return zz * 16 + jnp.where(core == 0, aa * 4 + bb, bb * 4 + aa)

    def peer_a(aa):
        return (s, at(zh, aa, b))

    def peer_b(bb):
        return (s, at(zh, a, bb))

    def owner(zz):
        return (s, at(zz, a, b))

    flip, mirror = a + 1 - 2 * (a % 2), 3 - a
    opposite = (a + 2) % 4

    def first_of(j):
        return jnp.where(j % 2 == 0, flip, mirror)

    def second_of(j):
        return jnp.where(j % 2 == 0, mirror, flip)

    barrier = pltpu.get_barrier_semaphore()

    def greet(device):
        pl.semaphore_signal(barrier, inc=1, device_id=device, device_id_type=MESH)

    greet(peer_a(flip))
    greet(peer_a(mirror))
    greet(peer_a(opposite))
    for o in (1, 2, 3):
        greet(peer_b((b + o) % 4))

        @pl.when(zh + o < 4)
        def _():
            greet(owner(zh + o))

    @pl.when(s > 0)
    def _():
        greet((s - 1, d))

    @pl.when(s < 3)
    def _():
        greet((s + 1, d))

    def part_at(j):
        return jnp.where(j == 3, zh, jnp.where(j < zh, j, j + 1))

    panel_part = jnp.where(zh == 0, 3, 0)
    first = 4 * panel_part + (8 - x - y) % 4

    def block_at(p):
        i = jnp.where(p == 0, first, jnp.where(p <= first, p - 1, p))
        return part_at(i // 4) * 4 + (i + x + y) % 4

    def columns(blk):
        return pl.ds(pl.multiple_of(blk * PANEL, PANEL), PANEL)

    def load(p, _):
        blk = block_at(p)

        @pl.when(s > 0)
        def _():
            pltpu.make_async_copy(x_hbm.at[:, columns(blk)], xbuf.at[blk], x_load).start()

        @pl.when(s == 3)
        def _():
            pltpu.make_async_copy(top_hbm.at[:, columns(blk)], cbuf.at[blk], c_in.at[blk]).start()

        return 0

    lax.fori_loop(0, BLOCKS, load, 0)
    pltpu.make_async_copy(gains_hbm, gains, gain_load).start()

    others = 6 + zh + jnp.where(s > 0, 1, 0) + jnp.where(s < 3, 1, 0)
    pl.semaphore_wait(barrier, others)

    for o in (1, 2, 3):

        @pl.when(zh >= o)
        def _():
            pl.semaphore_signal(above, inc=1, device_id=owner(zh - o), device_id_type=MESH)


    def swap(src, slot, aa):
        return pltpu.make_async_remote_copy(
            src_ref=src,
            dst_ref=held.at[slot, pl.ds(ROWS, ROWS), :],
            send_sem=swap_sent,
            recv_sem=swap_in.at[slot],
            device_id=peer_a(aa),
            device_id_type=MESH,
        )

    def keep(src, slot):
        return pltpu.make_async_copy(src, held.at[slot, pl.ds(0, ROWS), :], swap_in.at[slot])

    def is_panel(zz, q):
        return jnp.logical_and(core == 0, jnp.logical_and(zz == 0, q == 0))

    def other_than_panel(zz, q):
        return jnp.logical_not(is_panel(zz, q))

    def swap_part(j, piece):
        zz = part_at(j)
        to = first_of(j)
        for q, slot in ((opposite, 2 * j + 1), (to, 2 * j)):

            @pl.when(other_than_panel(zz, q))
            def _():
                swap(piece(zz * 4 + q), slot, to).start()

        for q, slot in ((second_of(j), 2 * j + 1), (a, 2 * j)):

            @pl.when(other_than_panel(zz, q))
            def _():
                keep(piece(zz * 4 + q), slot).start()

    def rows_of(aa):
        return pl.ds(pl.multiple_of(aa * ROWS, ROWS), ROWS)

    def hand(src, slot, aa):
        return pltpu.make_async_remote_copy(
            src_ref=src,
            dst_ref=gathered.at[slot, rows_of(a), :],
            send_sem=gather_sent,
            recv_sem=gather_in.at[slot],
            device_id=peer_a(aa),
            device_id_type=MESH,
        )

    def hold(src, slot):
        return pltpu.make_async_copy(src, gathered.at[slot, rows_of(a), :], gather_in.at[slot])

    def hand_part(j, piece):
        zz = part_at(j)
        for o in (2, 1, 3):
            aa = (a + o) % 4

            @pl.when(other_than_panel(zz, aa))
            def _():
                hand(piece(zz * 4 + aa), j, aa).start()

        @pl.when(other_than_panel(zz, a))
        def _():
            hold(piece(zz * 4 + a), j).start()

    def sort_part(f, j):
        zz = part_at(j)

        def sort(i, _):
            rows = pl.ds(pl.multiple_of(i * SORTED, SORTED), SORTED)
            blocks = [whole[f, zz * 4 + yy, rows, :].astype(F32) for yy in range(4)]
            for xx in range(4):
                sorted_by_x[f, zz * 4 + xx, rows, :] = jnp.concatenate(
                    [block[:, xx * 96 : xx * 96 + 96] for block in blocks], axis=1
                ).astype(BF16)
            return 0

        lax.fori_loop(0, ROWS // SORTED, sort, 0)

    x_panel = x_hbm.at[:, pl.ds(0, PANEL)]
    swap(x_panel, 8, flip).start()
    swap(x_panel, 9, mirror).start()
    keep(x_panel, 8).start()
    keep(x_panel, 9).start()

    def swap_x(j):
        @pl.when(core == 0)
        def _():
            swap_part(j, lambda blk: x_hbm.at[:, columns(blk)])

        @pl.when(core == 1)
        def _():
            sort_part(0, j)
            swap_part(j, lambda blk: sorted_by_x.at[0, blk])

    @pl.when(s > 0)
    def _():
        pltpu.make_async_copy(xbuf, xbuf, x_load).wait()

    pltpu.make_async_copy(gains_hbm, gains, gain_load).wait()

    def relay_copy(blk):
        return pltpu.make_async_remote_copy(
            src_ref=obuf.at[blk],
            dst_ref=cbuf.at[blk],
            send_sem=relay_sent,
            recv_sem=c_in.at[blk],
            device_id=(s - 1, d),
            device_id_type=MESH,
        )

    def relay(p, _):
        blk = block_at(p)
        pltpu.make_async_copy(cbuf.at[blk], cbuf.at[blk], c_in.at[blk]).wait()

        @pl.when(p == 0)
        def _():
            for o in (2, 1, 3):
                hand(cbuf.at[blk], 4, (a + o) % 4).start()
            hold(cbuf.at[blk], 4).start()

        @pl.when(s > 0)
        def _():
            gain = gains[blk]

            def slab(i, _):
                rows = pl.ds(pl.multiple_of(i * SLAB, SLAB), SLAB)
                scaling = 1.0 + gain * gelu_slope(xbuf[blk, rows, :].astype(F32))
                obuf[blk, rows, :] = (cbuf[blk, rows, :].astype(F32) * scaling).astype(BF16)
                return 0

            lax.fori_loop(0, ROWS // SLAB, slab, 0)
            relay_copy(blk).start()

        return 0

    def hand_c(j):
        @pl.when(core == 0)
        def _():
            hand_part(j, lambda blk: cbuf.at[blk])

        @pl.when(core == 1)
        def _():
            sort_part(1, j)
            hand_part(j, lambda blk: sorted_by_x.at[1, blk])

    def await_swap(slot):
        pltpu.make_async_copy(held.at[slot], held.at[slot], swap_in.at[slot]).wait()

    def await_gather(slot):
        pltpu.make_async_copy(gathered.at[slot], gathered.at[slot], gather_in.at[slot]).wait()

    def product(left, right):
        return lax.dot_general(left, right, (((0,), (0,)), ((), ())), preferred_element_type=F32)

    def a_copy(j):
        return pltpu.make_async_remote_copy(
            src_ref=asend.at[j],
            dst_ref=arecv.at[j],
            send_sem=a_sent,
            recv_sem=a_in.at[j],
            device_id=peer_a(second_of(j)),
            device_id_type=MESH,
        )

    def gram_x(j):
        zz = part_at(j)
        panel = 8 + j % 2

        @pl.when(j < 2)
        def _():
            await_swap(panel)

        def piece(q, slot):
            @pl.when(other_than_panel(zz, q))
            def _():
                await_swap(slot)

            return product(held[jnp.where(is_panel(zz, q), panel, slot)], held[panel])

        asend[j] = piece(second_of(j), 2 * j + 1).astype(BF16)
        a_copy(j).start()
        part[0, j] = piece(a, 2 * j)

    def gram_c(j):
        zz = part_at(j)

        @pl.when(j == 0)
        def _():
            await_gather(4)

        @pl.when(other_than_panel(zz, a))
        def _():
            await_gather(j)

        part[1, j] = product(gathered[jnp.where(is_panel(zz, a), 4, j)], gathered[4])
        for bb in range(4):
            bsend[1, j, bb] = part[1, j, pl.ds(bb * 96, 96), :].astype(BF16)
        for o in (2, 1, 3):
            b_copy(1, j, o).start()

    def b_copy(f, j, o):
        bb = (b + o) % 4
        return pltpu.make_async_remote_copy(
            src_ref=bsend.at[f, j, bb],
            dst_ref=brecv.at[f, j, o - 1],
            send_sem=b_sent.at[f],
            recv_sem=b_in.at[f, j],
            device_id=peer_b(bb),
            device_id_type=MESH,
        )

    def sum_a(j):
        a_copy(j).wait_recv()
        for bb in range(4):
            rows = pl.ds(bb * 96, 96)
            total = part[0, j, rows, :] + arecv[j, rows, :].astype(F32)
            part[0, j, rows, :] = total
            bsend[0, j, bb] = total.astype(BF16)
        for o in (2, 1, 3):
            b_copy(0, j, o).start()

    def c_copy(f, j):
        zz = part_at(j)
        return pltpu.make_async_remote_copy(
            src_ref=csend.at[f, j],
            dst_ref=crecv.at[f, jnp.where(zh < zz, zh, zh - 1)],
            send_sem=c_sent.at[f],
            recv_sem=c_got.at[f],
            device_id=owner(zz),
            device_id_type=MESH,
        )

    def meet_above():
        @pl.when(zh < 3)
        def _():
            pl.semaphore_wait(above, 3 - zh)

    def sum_b(f, j):
        pltpu.make_async_copy(brecv.at[f, j], brecv.at[f, j], b_in.at[f, j]).wait()
        total = part[f, j, pl.ds(pl.multiple_of(b * 96, 96), 96), :]
        for o in (1, 3, 2):
            total = total + brecv[f, j, o - 1].astype(F32)

        @pl.when(j == 3)
        def _():
            fin[f] = total

        @pl.when(j < 3)
        def _():
            csend[f, j] = total.astype(BF16)
            c_copy(f, j).start()

    def finish(f, out):
        pltpu.make_async_copy(crecv.at[f], crecv.at[f], c_got.at[f]).wait()
        total = fin[f]
        for j in range(3):
            total = total + crecv[f, j].astype(F32)
        out[...] = total

    words = [
        jnp.where(s == 0, w0, jnp.where(s == 1, w1, jnp.where(s == 2, w2, w3)))
        for w0, w1, w2, w3 in zip(*map(packed, (SECTION0, SECTION1, SECTION2, SECTION3)))
    ]

    def step(t, done):
        word = words[-1]
        for i in range(len(words) - 1):
            word = jnp.where(t // 3 == i, words[i], word)
        op = jnp.where(t % 3 == 0, word, jnp.where(t % 3 == 1, word // 256, word // 65536)) % 256
        kind, what = op // 32, op % 32
        upto = jnp.where(kind == RELAY, what, done)
        lax.fori_loop(done, upto, relay, 0)

        @pl.when(kind == HAND_C)
        def _():
            hand_c(what)

        @pl.when(kind == SWAP_X)
        def _():
            swap_x(what)

        @pl.when(kind == GRAM_X)
        def _():
            gram_x(what)

        @pl.when(kind == GRAM_C)
        def _():
            gram_c(what)

        @pl.when(kind == SUM_A)
        def _():
            sum_a(what)

        @pl.when(kind == MEET)
        def _():
            meet_above()

        @pl.when(kind == SUM_B)
        def _():
            sum_b(what // 4, what % 4)

        return upto

    lax.fori_loop(0, 3 * len(words), step, jnp.int32(0))
    finish(0, in_out)
    finish(1, grad_out)

    def await_sent(ref, sem):
        pltpu.make_async_copy(ref, ref, sem).wait()

    swaps = jnp.logical_and(core == 0, jnp.logical_and(a != 0, second_of(panel_part) != 0))
    hands = jnp.logical_and(core == 0, a != 0)
    for less, count, sem in ((swaps, 10, swap_sent), (hands, 15, gather_sent)):

        @pl.when(less)
        def _():
            await_sent(xbuf.at[pl.ds(0, count - 1)], sem)

        @pl.when(jnp.logical_not(less))
        def _():
            await_sent(xbuf.at[pl.ds(0, count)], sem)

    await_sent(asend, a_sent)
    for f in range(2):
        await_sent(bsend.at[f, pl.ds(0, 3)], b_sent.at[f])
        await_sent(csend.at[f], c_sent.at[f])

    @pl.when(s > 0)
    def _():
        await_sent(obuf, relay_sent)


def body(activations, top_cotangent, branch_gains):
    width = activations.shape[-1]
    total_rows = ROWS * lax.axis_size("dp")
    dma = pltpu.SemaphoreType.DMA
    sums = pl.pallas_call(
        kernel,
        out_shape=[jax.ShapeDtypeStruct((96, PANEL), F32)] * 2,
        in_specs=[
            pl.BlockSpec(memory_space=pl.ANY),
            pl.BlockSpec(memory_space=pl.ANY),
            pl.BlockSpec(memory_space=pl.ANY),
        ],
        out_specs=[pl.BlockSpec(memory_space=pltpu.VMEM)] * 2,
        scratch_shapes=[
            pltpu.VMEM((BLOCKS, 1, PANEL), F32),
            pltpu.VMEM((2, BLOCKS, ROWS, PANEL), BF16),
            pltpu.VMEM((2, BLOCKS, ROWS, PANEL), BF16),
            pltpu.VMEM((BLOCKS, ROWS, PANEL), BF16),
            pltpu.VMEM((10, 2 * ROWS, PANEL), BF16),
            pltpu.VMEM((5, 4 * ROWS, PANEL), BF16),
            pltpu.VMEM((2, 4, PANEL, PANEL), F32),
            pltpu.VMEM((4, PANEL, PANEL), BF16),
            pltpu.VMEM((4, PANEL, PANEL), BF16),
            pltpu.VMEM((2, 4, 4, 96, PANEL), BF16),
            pltpu.VMEM((2, 4, 3, 96, PANEL), BF16),
            pltpu.VMEM((2, 3, 96, PANEL), BF16),
            pltpu.VMEM((2, 3, 96, PANEL), BF16),
            pltpu.VMEM((2, 96, PANEL), F32),
            dma,
            dma,
            dma((BLOCKS,)),
            dma,
            dma,
            dma((10,)),
            dma,
            dma((5,)),
            dma,
            dma((4,)),
            dma((2,)),
            dma((2, 4)),
            dma((2,)),
            dma((2,)),
            pltpu.SemaphoreType.REGULAR,
        ],
        compiler_params=pltpu.CompilerParams(
            collective_id=0, has_side_effects=True, vmem_limit_bytes=56 * 2**20
        ),
        cost_estimate=pl.CostEstimate(
            flops=4 * ROWS * width * PANEL,
            bytes_accessed=4 * ROWS * width,
            transcendentals=2 * ROWS * width,
        ),
    )(
        activations.reshape(ROWS, width),
        top_cotangent.reshape(ROWS, width),
        branch_gains.reshape(BLOCKS, 1, PANEL),
    )
    return tuple((total / F32(total_rows))[None] for total in sums)


def solution(mesh):
    in_specs = (P("section", None, "dp", None), P(None, "dp", None), P("section", None))
    out_specs = (P("section", "dp", None), P("section", "dp", None))
    return jax.shard_map(
        body,
        mesh=mesh,
        in_specs=in_specs,
        out_specs=out_specs,
        check_vma=False,
    )
```

time: 73.3 us -> 66.2 us (0.903)
  the two profiles are of different devices: /device:TPU:80 before, /device:TPU:16 now
where the time goes in v3:
time: 66.2 us; the launch traced here: 65 us
  Pallas kernels  62.6 us (95%)
  other arithmetic  1.72 us (3%)
    pallas_call x1, Pallas kernels, body(): pl.pallas_call(kernel, out_shape=[jax.ShapeDtypeStruct((96, PANEL), F32)]...  62.6 us
    broadcast_in_dim x1, other arithmetic, body(): return tuple(((total / F32(total_rows))[None] for total in sums))  1.72 us

profile of v3, /device:TPU:16, one launch (start us, length us, event | category | flops | bytes accessed | tf_op | source)
XLA Modules:
  0.0 65.0 jit_solution(10143185711171534854)
XLA Ops:
  0.6 62.6 %shard_map.50 = (f32[96,384]{1,0:T(8,128)}, f32[96,384]{1,0:T(8,128)}) custom-call(bf16[224,6144]{1,0:T(8,128)(2,1)} %bitcast.7, bf16[224,6144]{1,0:T(8,128)(2,1)} %bitcast.8, f32[16,1,384]{2,1,0:T(1,128)} %bitcast.9), custom_call_target="tpu_custom_call" | custom-call | flops 2113929216 | bytes 5505024 | tf_op jit(solution)/shard_map/pallas_call | solution.py:499
  63.3 1.7 %multiply_bitcast_fusion = (f32[1,96,384]{2,1,0:T(8,128)}, f32[1,96,384]{2,1,0:T(8,128)}) fusion(f32[96,384]{1,0:T(8,128)} %get-tuple-element.5, f32[96,384]{1,0:T(8,128)} %get-tuple-element.4), kind=kLoop, calls=%fused_computation | loop fusion | flops 73728 | bytes 589824 | tf_op jit(solution)/shard_map/broadcast_in_dim | solution.py:552

commit v4 on v3

--- a/solution.py
+++ b/solution.py
@@ -12,10 +12,10 @@
 SORTED = 112
 KINDS = RELAY, HAND_C, GRAM_X, GRAM_C, SUM_A, SUM_B, MEET, SWAP_X = range(8)
 R, S, G, D, A, B, M, X = (32 * kind for kind in KINDS)
-SECTION3 = (R + 2, X + 0, R + 4, X + 1, R + 6, X + 2, R + 8, X + 3, R + 16, G + 0, G + 1, S + 0, S + 1, G + 2, G + 3, S + 2, S + 3, A + 0, A + 1, A + 2, A + 3, D + 0, D + 1, M + 0, B + 0, B + 1, B + 2, B + 3, D + 2, D + 3, B + 4, B + 5, B + 6, B + 7)
-SECTION2 = (X + 0, X + 1, X + 2, X + 3, R + 16, G + 0, G + 1, S + 0, S + 1, G + 2, G + 3, S + 2, S + 3, A + 0, A + 1, A + 2, A + 3, D + 0, D + 1, M + 0, B + 0, B + 1, B + 2, B + 3, D + 2, D + 3, B + 4, B + 5, B + 6, B + 7)
-SECTION1 = (X + 0, X + 1, X + 2, X + 3, R + 4, G + 0, G + 1, R + 5, S + 0, G + 2, G + 3, R + 9, S + 1, A + 0, A + 1, D + 0, R + 10, A + 2, A + 3, R + 13, S + 2, D + 1, M + 0, B + 0, B + 1, B + 4, R + 16, S + 3, B + 2, B + 3, D + 2, B + 5, D + 3, B + 6, B + 7)
-SECTION0 = (X + 0, X + 1, X + 2, X + 3, R + 4, G + 0, G + 1, R + 5, S + 0, G + 2, G + 3, R + 9, S + 1, A + 0, A + 1, D + 0, R + 10, A + 2, A + 3, R + 13, S + 2, D + 1, M + 0, B + 0, B + 1, B + 4, R + 16, S + 3, B + 2, B + 3, D + 2, B + 5, D + 3, B + 6, B + 7)
+SECTION3 = (R + 2, X + 0, R + 4, X + 1, R + 6, X + 2, R + 8, X + 3, R + 16, G + 0, G + 1, G + 2, G + 3, S + 0, S + 1, A + 0, A + 1, A + 2, A + 3, S + 2, D + 0, S + 3, D + 1, M + 0, B + 0, B + 1, B + 2, B + 3, B + 4, D + 2, B + 5, D + 3, B + 6, B + 7)
+SECTION2 = (X + 0, X + 1, X + 2, X + 3, R + 16, G + 0, G + 1, G + 2, G + 3, S + 0, S + 1, A + 0, A + 1, A + 2, A + 3, S + 2, D + 0, S + 3, D + 1, M + 0, B + 0, B + 1, B + 2, B + 3, B + 4, D + 2, B + 5, D + 3, B + 6, B + 7)
+SECTION1 = (X + 0, X + 1, X + 2, X + 3, R + 4, G + 0, G + 1, R + 5, S + 0, G + 2, G + 3, R + 9, S + 1, A + 0, R + 10, A + 1, D + 0, A + 2, A + 3, R + 13, S + 2, D + 1, M + 0, B + 0, B + 1, B + 4, R + 16, S + 3, B + 2, B + 3, D + 2, B + 5, D + 3, B + 6, B + 7)
+SECTION0 = (X + 0, X + 1, X + 2, X + 3, R + 4, G + 0, G + 1, R + 5, S + 0, G + 2, G + 3, R + 9, S + 1, A + 0, R + 10, A + 1, D + 0, A + 2, A + 3, R + 13, S + 2, D + 1, M + 0, B + 0, B + 1, B + 4, R + 16, S + 3, B + 2, B + 3, D + 2, B + 5, D + 3, B + 6, B + 7)
 WORDS = 15
 MESH = pl.DeviceIdType.MESH
 F32 = jnp.float32
@@ -537,7 +537,7 @@
             pltpu.SemaphoreType.REGULAR,
         ],
         compiler_params=pltpu.CompilerParams(
-            collective_id=0, has_side_effects=True, vmem_limit_bytes=56 * 2**20
+            collective_id=0, has_side_effects=True, vmem_limit_bytes=53 * 2**20
         ),
         cost_estimate=pl.CostEstimate(
             flops=4 * ROWS * width * PANEL,

time: 66.2 us -> 63.9 us (0.965); the launches traced: 65 us -> 63.7 us
  Pallas kernels: 62.6 us -> 61.6 us
  other arithmetic: 1.72 us -> 0.74 us
  local copies, waits for them, and re-layouts: 0 us -> 0.73 us
    pallas_call x1, Pallas kernels: 62.6 us -> 61.6 us  [body(): pl.pallas_call(kernel, out_shape=[jax.ShapeDtypeStruct((96, PANEL), F32)]...]
    broadcast_in_dim x1, other arithmetic: 1.72 us -> 0.74 us  [body(): return tuple(((total / F32(total_rows))[None] for total in sums))]
    unnamed x0 -> x2, local copies, waits for them, and re-layouts: none -> 0.73 us
where the time goes in v4:
time: 63.9 us; the launch traced here: 63.7 us
  Pallas kernels  61.6 us (96%)
  other arithmetic  0.74 us (1%)
  local copies, waits for them, and re-layouts  0.73 us (1%)
  between operations  0.65 us (1%)
    pallas_call x1, Pallas kernels, body(): pl.pallas_call(kernel, out_shape=[jax.ShapeDtypeStruct((96, PANEL), F32)]...  61.6 us

profile of v4, /device:TPU:16, one launch (start us, length us, event | category | flops | bytes accessed | tf_op | source)
XLA Modules:
  0.0 63.7 jit_solution(10718724834054003236)
XLA Ops:
  0.6 0.0 copy-start
  0.6 0.7 %copy-done = f32[1,6144]{1,0:T(1,128)S(1)} copy-done((f32[1,6144]{1,0:T(1,128)S(1)}, f32[1,6144]{1,0:T(1,128)}, u32[]{:S(2)}) %copy-start) | copy-done | bytes 24600
  1.4 61.6 %shard_map.50 = (f32[96,384]{1,0:T(8,128)S(1)}, f32[96,384]{1,0:T(8,128)S(1)}) custom-call(bf16[224,6144]{1,0:T(8,128)(2,1)} %bitcast.8, bf16[224,6144]{1,0:T(8,128)(2,1)} %bitcast.9, f32[16,1,384]{2,1,0:T(1,128)S(1)} %bitcast.7), custom_call_target="tpu_custom_call" | custom-call | flops 2113929216 | bytes 5505024 | tf_op jit(solution)/shard_map/pallas_call | solution.py:499
  63.0 0.7 %multiply_bitcast_fusion = (f32[1,96,384]{2,1,0:T(8,128)}, f32[1,96,384]{2,1,0:T(8,128)}) fusion(f32[96,384]{1,0:T(8,128)S(1)} %get-tuple-element.5, f32[96,384]{1,0:T(8,128)S(1)} %get-tuple-element.4), kind=kLoop, calls=%fused_computation | loop fusion | flops 73728 | bytes 589824 | tf_op jit(solution)/shard_map/broadcast_in_dim | solution.py:552
Async XLA Ops:
  0.6 0.7 %copy-start = (f32[1,6144]{1,0:T(1,128)S(1)}, f32[1,6144]{1,0:T(1,128)}, u32[]{:S(2)}) copy-start(f32[1,6144]{1,0:T(1,128)} %param.5) | copy-start | bytes 73732

commit v5 on v4

--- a/solution.py
+++ b/solution.py
@@ -14,8 +14,8 @@
 R, S, G, D, A, B, M, X = (32 * kind for kind in KINDS)
 SECTION3 = (R + 2, X + 0, R + 4, X + 1, R + 6, X + 2, R + 8, X + 3, R + 16, G + 0, G + 1, G + 2, G + 3, S + 0, S + 1, A + 0, A + 1, A + 2, A + 3, S + 2, D + 0, S + 3, D + 1, M + 0, B + 0, B + 1, B + 2, B + 3, B + 4, D + 2, B + 5, D + 3, B + 6, B + 7)
 SECTION2 = (X + 0, X + 1, X + 2, X + 3, R + 16, G + 0, G + 1, G + 2, G + 3, S + 0, S + 1, A + 0, A + 1, A + 2, A + 3, S + 2, D + 0, S + 3, D + 1, M + 0, B + 0, B + 1, B + 2, B + 3, B + 4, D + 2, B + 5, D + 3, B + 6, B + 7)
-SECTION1 = (X + 0, X + 1, X + 2, X + 3, R + 4, G + 0, G + 1, R + 5, S + 0, G + 2, G + 3, R + 9, S + 1, A + 0, R + 10, A + 1, D + 0, A + 2, A + 3, R + 13, S + 2, D + 1, M + 0, B + 0, B + 1, B + 4, R + 16, S + 3, B + 2, B + 3, D + 2, B + 5, D + 3, B + 6, B + 7)
-SECTION0 = (X + 0, X + 1, X + 2, X + 3, R + 4, G + 0, G + 1, R + 5, S + 0, G + 2, G + 3, R + 9, S + 1, A + 0, R + 10, A + 1, D + 0, A + 2, A + 3, R + 13, S + 2, D + 1, M + 0, B + 0, B + 1, B + 4, R + 16, S + 3, B + 2, B + 3, D + 2, B + 5, D + 3, B + 6, B + 7)
+SECTION1 = (X + 0, X + 1, X + 2, X + 3, R + 4, G + 0, G + 1, R + 5, S + 0, G + 2, G + 3, R + 9, S + 1, A + 0, R + 10, A + 1, D + 0, A + 2, A + 3, R + 13, S + 2, D + 1, M + 0, B + 0, B + 1, B + 4, R + 16, S + 3, D + 2, B + 2, B + 3, B + 5, D + 3, B + 6, B + 7)
+SECTION0 = (X + 0, X + 1, X + 2, X + 3, R + 4, G + 0, G + 1, R + 5, S + 0, G + 2, G + 3, R + 9, S + 1, A + 0, R + 10, A + 1, D + 0, A + 2, A + 3, R + 13, S + 2, D + 1, M + 0, B + 0, B + 1, B + 4, R + 16, S + 3, D + 2, B + 2, B + 3, B + 5, D + 3, B + 6, B + 7)
 WORDS = 15
 MESH = pl.DeviceIdType.MESH
 F32 = jnp.float32

time: 63.9 us -> 63.9 us (level)
  no operation moved by 1% of the time
where the time goes in v5:
time: 63.9 us; the launch traced here: 63.7 us
  Pallas kernels  61.6 us (96%)
  other arithmetic  0.74 us (1%)
  local copies, waits for them, and re-layouts  0.73 us (1%)
  between operations  0.65 us (1%)
    pallas_call x1, Pallas kernels, body(): pl.pallas_call(kernel, out_shape=[jax.ShapeDtypeStruct((96, PANEL), F32)]...  61.6 us

profile of v5, /device:TPU:16, one launch (start us, length us, event | category | flops | bytes accessed | tf_op | source)
XLA Modules:
  0.0 63.7 jit_solution(16724988103924882145)
XLA Ops:
  0.6 0.0 copy-start
  0.6 0.7 %copy-done = f32[1,6144]{1,0:T(1,128)S(1)} copy-done((f32[1,6144]{1,0:T(1,128)S(1)}, f32[1,6144]{1,0:T(1,128)}, u32[]{:S(2)}) %copy-start) | copy-done | bytes 24600
  1.4 61.6 %shard_map.50 = (f32[96,384]{1,0:T(8,128)S(1)}, f32[96,384]{1,0:T(8,128)S(1)}) custom-call(bf16[224,6144]{1,0:T(8,128)(2,1)} %bitcast.8, bf16[224,6144]{1,0:T(8,128)(2,1)} %bitcast.9, f32[16,1,384]{2,1,0:T(1,128)S(1)} %bitcast.7), custom_call_target="tpu_custom_call" | custom-call | flops 2113929216 | bytes 5505024 | tf_op jit(solution)/shard_map/pallas_call | solution.py:499
  63.0 0.7 %multiply_bitcast_fusion = (f32[1,96,384]{2,1,0:T(8,128)}, f32[1,96,384]{2,1,0:T(8,128)}) fusion(f32[96,384]{1,0:T(8,128)S(1)} %get-tuple-element.5, f32[96,384]{1,0:T(8,128)S(1)} %get-tuple-element.4), kind=kLoop, calls=%fused_computation | loop fusion | flops 73728 | bytes 589824 | tf_op jit(solution)/shard_map/broadcast_in_dim | solution.py:552
Async XLA Ops:
  0.6 0.7 %copy-start = (f32[1,6144]{1,0:T(1,128)S(1)}, f32[1,6144]{1,0:T(1,128)}, u32[]{:S(2)}) copy-start(f32[1,6144]{1,0:T(1,128)} %param.5) | copy-start | bytes 73732
